TPU v7x, 256 devices: a whole 4x4x8 slice. The times are simulated.
256 devices in a mesh: ctx: 32 (over y, z), head: 8 (over x, core).
Axes of the slice: x: 4, y: 4, z: 8, core: 2. Of those that a mesh axis runs over, the one named last changes fastest.
Arguments:
- queries: bfloat16 [32768, 2048], P('ctx', 'head'), may hold values from -6 to 6
- key_vectors: bfloat16 [32768, 2048], P('ctx', 'head'), may hold values from -6 to 6
- value_vectors: bfloat16 [32768, 2048], P('ctx', 'head'), may hold values from -60 to 60
- write_rates: float32 [32768, 16], P('ctx', 'head'), may hold values from 0 to 1
- doc_lengths: int32 [32], replicated, may hold values from 1 to 16384, 32768 in all
- norm_gain: float32 [2048], P('head'), may hold values from 0.5 to 1.5
Outputs:
- normed: bfloat16 [32768, 2048], P('ctx', 'head')
All inputs are finite; a program needn't handle non-finite values.
Results may differ from a plain program's by a relative error of at most 0.0014.
Values sent between devices are 32-bit elements; how exact they have to be, the bound alone decides.
A program may use at most 64 MiB of HBM per device.

v0:
```python
import jax
import jax.numpy as jnp
from jax import lax
from jax.sharding import PartitionSpec as P

BLOCK = 128
highest = lax.Precision.HIGHEST
epsilon = 1e-06


def entering(part, axis, combine, identity):
    place = lax.axis_index(axis)
    gathered = jax.tree.map(lambda a: lax.all_gather(a, axis), part)
    state = jax.tree.map(lambda a, e: jnp.zeros_like(a) + jnp.asarray(e, a.dtype), part, identity)

    def one(lap, state):
        return combine(
            state, jax.tree.map(lambda a: lax.dynamic_index_in_dim(a, lap, 0, False), gathered)
        )

    return lax.fori_loop(0, place, one, state)


def normalize(rows):
    return rows * lax.rsqrt(jnp.sum(rows * rows, axis=-1, keepdims=True) + epsilon)


def document_ids(doc_lengths, positions):
    ends = jnp.cumsum(doc_lengths, dtype=jnp.int32)
    begins = ends - doc_lengths
    return jnp.sum((begins[None, :] <= positions[:, None]).astype(jnp.int32), axis=1) - 1


def combine_pairs(earlier, later):
    mul_early, add_early = earlier
    mul_late, add_late = later
    product = jnp.einsum("hij,hjk->hik", mul_late, mul_early, precision=highest)
    shifted = jnp.einsum("hij,hjk->hik", mul_late, add_early, precision=highest) + add_late
    return (product, shifted)


def local(queries, key_vectors, value_vectors, write_rates, doc_lengths, norm_gain):
    tok_dev = queries.shape[0]
    head_count = write_rates.shape[1]
    head_dim = queries.shape[1] // head_count
    block_count = tok_dev // BLOCK

    def split_heads(matrix):
        return (
            matrix.astype(jnp.float32)
            .reshape(block_count, BLOCK, head_count, head_dim)
            .transpose(0, 2, 1, 3)
        )

    query_blocks = normalize(split_heads(queries))
    key_blocks = normalize(split_heads(key_vectors))
    value_blocks = split_heads(value_vectors)
    rate_blocks = write_rates.reshape(block_count, BLOCK, head_count).transpose(0, 2, 1)
    offset = lax.axis_index("ctx") * tok_dev
    positions = offset + jnp.arange(tok_dev, dtype=jnp.int32)
    doc_here = document_ids(doc_lengths, positions).reshape(block_count, BLOCK)
    block_begin = offset + jnp.arange(block_count, dtype=jnp.int32) * BLOCK - 1
    doc_before = document_ids(doc_lengths, block_begin)
    carry_mask = (doc_here == doc_before[:, None]).astype(jnp.float32)
    last_mask = (doc_here == doc_here[:, -1:]).astype(jnp.float32)
    same_doc = doc_here[:, None, :, None] == doc_here[:, None, None, :]
    rows_index = jnp.arange(BLOCK)
    lower_strict = rows_index[:, None] > rows_index[None, :]
    lower_incl = rows_index[:, None] >= rows_index[None, :]
    key_gram = jnp.einsum("nhcd,nhed->nhce", key_blocks, key_blocks, precision=highest)
    coupling = jnp.where(lower_strict & same_doc, rate_blocks[..., :, None] * key_gram, 0.0)
    system = coupling + jnp.eye(BLOCK, dtype=jnp.float32)
    stacked = jnp.concatenate([key_blocks, value_blocks], axis=-1) * rate_blocks[..., None]
    solved = jax.scipy.linalg.solve_triangular(system, stacked, lower=True, unit_diagonal=True)
    wy_keys = solved[..., :head_dim]
    wy_values = solved[..., head_dim:]
    scores = jnp.einsum("nhcd,nhed->nhce", query_blocks, key_blocks, precision=highest)
    scores = jnp.where(lower_incl & same_doc, scores, 0.0)
    carried_keys = wy_keys * carry_mask[:, None, :, None]
    last_keys = key_blocks * last_mask[:, None, :, None]
    carried_queries = query_blocks * carry_mask[:, None, :, None]
    carry_last = carry_mask[:, -1]
    identity_mat = jnp.broadcast_to(
        jnp.eye(head_dim, dtype=jnp.float32), (head_count, head_dim, head_dim)
    )
    zero_state = jnp.zeros((head_count, head_dim, head_dim), jnp.float32)
    step_mul = carry_last[:, None, None, None] * identity_mat[None] - jnp.einsum(
        "nhcd,nhce->nhde", last_keys, carried_keys, precision=highest
    )
    step_add = jnp.einsum("nhcd,nhce->nhde", last_keys, wy_values, precision=highest)

    def fold_pairs(pair, block_pair):
        return (combine_pairs(pair, block_pair), None)

    (dev_mul, dev_add), _ = lax.scan(fold_pairs, (identity_mat, zero_state), (step_mul, step_add))
    _, entry_state = entering((dev_mul, dev_add), "ctx", combine_pairs, (identity_mat, zero_state))

    def run_one(state, block):
        query_now, score_now, carried_now, value_now, last_now, keep_now = block
        updated = value_now - jnp.einsum("hcd,hde->hce", carried_now, state, precision=highest)
        output = jnp.einsum("hcd,hde->hce", query_now, state, precision=highest)
        output = output + jnp.einsum("hce,hed->hcd", score_now, updated, precision=highest)
        state = keep_now * state + jnp.einsum("hcd,hce->hde", last_now, updated, precision=highest)
        return (state, output)

    _, outputs = lax.scan(
        run_one,
        entry_state,
        (carried_queries, scores, carried_keys, wy_values, last_keys, carry_last),
    )
    outputs = outputs.transpose(0, 2, 1, 3).reshape(tok_dev, head_count * head_dim)
    local_squares = jnp.sum(outputs * outputs, axis=1)
    total_squares = lax.psum(local_squares, "head")
    width_all = head_count * head_dim * lax.axis_size("head")
    scale = lax.rsqrt(total_squares / width_all + epsilon)
    return (outputs * scale[:, None] * norm_gain[None, :]).astype(jnp.bfloat16)


def solution(mesh):
    placed = (
        P("ctx", "head"),
        P("ctx", "head"),
        P("ctx", "head"),
        P("ctx", "head"),
        P(),
        P("head"),
    )
    return jax.shard_map(
        local, mesh=mesh, in_specs=placed, out_specs=P("ctx", "head"), check_vma=False
    )
```

profile of v0, /device:TPU:249, one launch (start us, length us, event | category | flops | bytes accessed | tf_op | source)
XLA Modules:
  0.0 490.3 jit_solution(16350187449445751479)
XLA Ops:
  19.4 4.1 fusion.35
  23.5 158.6 %custom-call.4 = f32[8,2,1,128,128]{3,4,2,1,0:T(8,128)} custom-call(f32[8,2,1,128,128]{4,3,2,1,0:T(8,128)} %fusion.35), custom_call_target="InvertDiagBlocksLowerTriangular" | custom-call | tf_op jit(solution)/shard_map/jit(_solve_triangular)/vmap(vmap())/triangular_solve | solution.py:74
  182.1 2.5 reshape.193
  184.7 2.5 copy.108
  187.2 1.8 maximum_multiply_fusion
  189.1 2.3 fusion.29
  191.4 2.3 fusion.47
  193.7 1.9 fusion.51
  196.6 2.3 convolution_subtract_fusion.1
  199.0 19.9 %while.42 = (s32[]{:T(128)}, f32[2,128,128]{2,1,0:T(8,128)S(1)}, f32[2,128,128]{2,1,0:T(8,128)S(1)}, f32[8,2,128,128]{3,2,1,0:T(8,128)}, f32[8,2,128,128]{3,2,1,0:T(8,128)}) while((s32[]{:T(128)}, f32[2,128,128]{2,1,0:T(8,128)S(1)}, f32[2,128,128]{2,1,0:T(8,128)S(1)}, f32[8,2,128,128]{3,2,1,0:T(8,128)}, ...), condition=%wide.region_5.6_spmd.clone.clone, body=%wide.region_4.5_spmd.clone.sunk.clone | while | flops 100728832 | bytes 1443410 | solution.py:95
  221.4 3.3 convolution_select_fusion
  224.8 70.8 %all-gather.7.cloned.1.call-done = f32[64,128,128]{2,1,0:T(8,128)} async-done(((f32[2,128,128]{2,1,0:T(8,128)}), f32[64,128,128]{2,1,0:T(8,128)}) %all-gather.7.cloned.1.call-update) | async-done | bytes 4194320 | tf_op jit(solution)/shard_map/all_gather | solution.py:13
  295.5 81.7 %all-gather.5.cloned.1.call-done = f32[64,128,128]{2,1,0:T(8,128)} async-done(((f32[2,128,128]{2,1,0:T(8,128)}), f32[64,128,128]{2,1,0:T(8,128)}) %all-gather.5.cloned.1.call-update) | async-done | bytes 4194320 | tf_op jit(solution)/shard_map/all_gather | solution.py:13
  377.2 39.9 %while.40 = (s32[]{:T(128)}, f32[2,128,128]{2,1,0:T(8,128)S(1)}, s32[]{:T(128)}, f32[32,2,128,128]{3,2,1,0:T(8,128)}, f32[32,2,128,128]{3,2,1,0:T(8,128)}) while((s32[]{:T(128)}, f32[2,128,128]{2,1,0:T(8,128)S(1)}, s32[]{:T(128)}, f32[32,2,128,128]{3,2,1,0:T(8,128)}, f32[32,2,128,128]{3,2,1,0:T(8,128)}) %tuple.87), condition=%wide.region_7.8_spmd.clone, body=%wide.region_6.7_spmd.sunk.clone | while | flops 50364420 | bytes 787559 | solution.py:21
  417.1 48.3 %while.41 = (s32[]{:T(128)}, f32[2,128,128]{2,1,0:T(8,128)S(1)}, f32[8,2,128,128]{3,2,1,0:T(8,128)S(1)}, f32[8]{0:T(128)S(1)}, f32[8,2,128,128]{2,3,1,0:T(8,128)...) while((s32[]{:T(128)}, f32[2,128,128]{2,1,0:T(8,128)S(1)}, ...), condition=%wide.region_10.11_spmd.clone, body=%wide.region_9.10_spmd.sunk.clone | while | flops 201457664 | bytes 1968761 | solution.py:106
  420.1 1.8 convolution_add_fusion.11
  426.2 1.8 convolution_add_fusion.11
  432.2 1.8 convolution_add_fusion.11
  438.3 1.8 convolution_add_fusion.11
  444.3 1.8 convolution_add_fusion.11
  450.4 1.8 convolution_add_fusion.11
  456.4 1.8 convolution_add_fusion.11
  462.4 1.8 convolution_add_fusion.11
  465.7 15.9 %psum.7 = f32[1024]{0:T(1024)S(1)} all-reduce(f32[1024]{0:T(1024)S(1)} %bitcast.145), channel_id=1, replica_groups=mesh['ctx'=32,'head'=8] {'head'}, use_global_device_ids=true, to_apply=%region_12.13 | all-reduce | flops 1024 | bytes 8192 | tf_op jit(solution)/shard_map/psum | solution.py:113
  (186 shorter events, 110.1 us)
Async XLA Ops:
  6.5 7.5 %copy-start.4 = (bf16[1024,256]{1,0:T(8,128)(2,1)S(1)}, bf16[1024,256]{1,0:T(8,128)(2,1)}, u32[]{:S(2)}) copy-start(bf16[1024,256]{1,0:T(8,128)(2,1)} %param.13) | copy-start | bytes 1572868
  6.5 289.0 %all-gather.7.cloned.1.call-start = ((), (), s32[]{:S(2)}) async-start(), calls=%async_computation.1 | async-start | bytes 4325376 | tf_op jit(solution)/shard_map/all_gather | solution.py:13
  23.5 163.7 %copy-start.6 = (f32[8,2,128]{2,0,1:T(8,128)S(1)}, f32[8,2,128]{2,0,1:T(8,128)}, u32[]{:S(2)}) copy-start(f32[8,2,128]{2,0,1:T(8,128)} %copy.94) | copy-start | bytes 24580
  187.2 1.9 copy-start.3
  193.7 2.9 copy-start.7
  195.6 1.0 copy-start
  218.8 0.7 copy-start.2
  218.8 0.7 copy-start.1
  218.9 2.6 copy-start.5
  219.5 157.7 %all-gather.5.cloned.1.call-start = ((), (), s32[]{:S(2)}) async-start(), calls=%async_computation | async-start | bytes 4325376 | tf_op jit(solution)/shard_map/all_gather | solution.py:13
  465.5 17.0 %copy-start.8 = (f32[256]{0:T(256)S(1)}, f32[256]{0:T(256)}, u32[]{:S(2)}) copy-start(f32[256]{0:T(256)} %param.17) | copy-start | bytes 3076
Sparse Core Ops, SparseCore 0:
  219.6 75.8 all-gather.6
  298.1 79.0 all-gather.4
where the time goes:
time: 492 us; the launch traced here: 490 us
  other arithmetic  169 us (34%)
  waiting for transfers between devices  153 us (31%)
  matrix products  115 us (23%)
  local copies, waits for them, and re-layouts  21 us (4%)
  blocking collectives  15.9 us (3%)
  between operations  13.6 us (3%)
    another operation x4, other arithmetic, local(): jax.scipy.linalg.solve_triangular(system, stacked, lower=True, unit_diago...  159 us
    all_gather x2, waiting for transfers between devices, entering(): gathered = jax.tree.map(lambda a: lax.all_gather(a, axis), part)  152 us
    dot_general x39, matrix products, combine_pairs(): jnp.einsum('hij,hjk->hik', mul_late, add_early, precision=highest)  48.4 us
    psum x1, blocking collectives, local(): total_squares = lax.psum(local_squares, 'head')  15.9 us
    dot_general x8, matrix products, run_one(): jnp.einsum('hcd,hce->hde', last_now, updated, precision=highest)  14.6 us
    dot_general x8, matrix products, run_one(): jnp.einsum('hcd,hde->hce', carried_now, state, precision=highest)  9.86 us
  transfers between devices with their start and end apart: 2, of which 2 were waited for; matrix products, arithmetic and copies ran while one was open for 1% of the time, Pallas kernels for 0%

commit v1 on v0

--- a/solution.py
+++ b/solution.py
@@ -110,7 +110,7 @@
     )
     outputs = outputs.transpose(0, 2, 1, 3).reshape(tok_dev, head_count * head_dim)
     local_squares = jnp.sum(outputs * outputs, axis=1)
-    total_squares = lax.psum(local_squares, "head")
+    total_squares = jnp.sum(lax.all_gather(local_squares, "head"), axis=0)
     width_all = head_count * head_dim * lax.axis_size("head")
     scale = lax.rsqrt(total_squares / width_all + epsilon)
     return (outputs * scale[:, None] * norm_gain[None, :]).astype(jnp.bfloat16)

time: 492 us -> 494 us (level)
    all_gather x0 -> x1, blocking collectives: none -> 17 us  [local(): total_squares = jnp.sum(lax.all_gather(local_squares, 'head'), axis=0)]
    psum x1 -> x0, blocking collectives: 15.9 us -> none  [local(): total_squares = lax.psum(local_squares, 'head')]
where the time goes in v1:
time: 494 us; the launch traced here: 492 us
  other arithmetic  169 us (34%)
  waiting for transfers between devices  153 us (31%)
  matrix products  115 us (23%)
  local copies, waits for them, and re-layouts  21 us (4%)
  blocking collectives  17 us (3%)
  between operations  13.6 us (3%)
    another operation x4, other arithmetic, local(): jax.scipy.linalg.solve_triangular(system, stacked, lower=True, unit_diago...  159 us
    all_gather x2, waiting for transfers between devices, entering(): gathered = jax.tree.map(lambda a: lax.all_gather(a, axis), part)  152 us
    dot_general x39, matrix products, combine_pairs(): jnp.einsum('hij,hjk->hik', mul_late, add_early, precision=highest)  48.4 us
    all_gather x1, blocking collectives, local(): total_squares = jnp.sum(lax.all_gather(local_squares, 'head'), axis=0)  17 us
    dot_general x8, matrix products, run_one(): jnp.einsum('hcd,hce->hde', last_now, updated, precision=highest)  14.6 us
  transfers between devices with their start and end apart: 2, of which 2 were waited for; matrix products, arithmetic and copies ran while one was open for 1% of the time, Pallas kernels for 0%

profile of v1, /device:TPU:249, one launch (start us, length us, event | category | flops | bytes accessed | tf_op | source)
XLA Modules:
  0.0 491.7 jit_solution(11008018842772264741)
XLA Ops:
  19.4 4.1 fusion.35
  23.5 158.6 %custom-call.4 = f32[8,2,1,128,128]{3,4,2,1,0:T(8,128)} custom-call(f32[8,2,1,128,128]{4,3,2,1,0:T(8,128)} %fusion.35), custom_call_target="InvertDiagBlocksLowerTriangular" | custom-call | tf_op jit(solution)/shard_map/jit(_solve_triangular)/vmap(vmap())/triangular_solve | solution.py:74
  182.1 2.5 reshape.201
  184.7 2.5 copy.108
  187.2 1.8 maximum_multiply_fusion
  189.1 2.3 fusion.29
  191.4 2.3 fusion.47
  193.7 1.9 fusion.51
  196.6 2.3 convolution_subtract_fusion.1
  199.0 19.9 %while.42 = (s32[]{:T(128)}, f32[2,128,128]{2,1,0:T(8,128)S(1)}, f32[2,128,128]{2,1,0:T(8,128)S(1)}, f32[8,2,128,128]{3,2,1,0:T(8,128)}, f32[8,2,128,128]{3,2,1,0:T(8,128)}) while((s32[]{:T(128)}, f32[2,128,128]{2,1,0:T(8,128)S(1)}, f32[2,128,128]{2,1,0:T(8,128)S(1)}, f32[8,2,128,128]{3,2,1,0:T(8,128)}, ...), condition=%wide.region_5.6_spmd.clone.clone, body=%wide.region_4.5_spmd.clone.sunk.clone | while | flops 100728832 | bytes 1443410 | solution.py:95
  221.4 3.3 convolution_select_fusion
  224.8 70.8 %all-gather.8.cloned.1.call-done = f32[64,128,128]{2,1,0:T(8,128)} async-done(((f32[2,128,128]{2,1,0:T(8,128)}), f32[64,128,128]{2,1,0:T(8,128)}) %all-gather.8.cloned.1.call-update) | async-done | bytes 4194320 | tf_op jit(solution)/shard_map/all_gather | solution.py:13
  295.5 81.7 %all-gather.6.cloned.1.call-done = f32[64,128,128]{2,1,0:T(8,128)} async-done(((f32[2,128,128]{2,1,0:T(8,128)}), f32[64,128,128]{2,1,0:T(8,128)}) %all-gather.6.cloned.1.call-update) | async-done | bytes 4194320 | tf_op jit(solution)/shard_map/all_gather | solution.py:13
  377.2 39.9 %while.40 = (s32[]{:T(128)}, f32[2,128,128]{2,1,0:T(8,128)S(1)}, s32[]{:T(128)}, f32[32,2,128,128]{3,2,1,0:T(8,128)}, f32[32,2,128,128]{3,2,1,0:T(8,128)}) while((s32[]{:T(128)}, f32[2,128,128]{2,1,0:T(8,128)S(1)}, s32[]{:T(128)}, f32[32,2,128,128]{3,2,1,0:T(8,128)}, f32[32,2,128,128]{3,2,1,0:T(8,128)}) %tuple.87), condition=%wide.region_7.8_spmd.clone, body=%wide.region_6.7_spmd.sunk.clone | while | flops 50364420 | bytes 787559 | solution.py:21
  417.1 48.6 %while.41 = (s32[]{:T(128)}, f32[2,128,128]{2,1,0:T(8,128)S(1)}, f32[8,2,128,128]{3,2,1,0:T(8,128)S(1)}, f32[8]{0:T(128)S(1)}, f32[8,2,128,128]{2,3,1,0:T(8,128)...) while((s32[]{:T(128)}, f32[2,128,128]{2,1,0:T(8,128)S(1)}, ...), condition=%wide.region_10.11_spmd.clone, body=%wide.region_9.10_spmd.sunk.clone | while | flops 201457664 | bytes 1968761 | solution.py:106
  420.4 1.8 convolution_add_fusion.11
  426.4 1.8 convolution_add_fusion.11
  432.4 1.8 convolution_add_fusion.11
  438.5 1.8 convolution_add_fusion.11
  444.5 1.8 convolution_add_fusion.11
  450.6 1.8 convolution_add_fusion.11
  456.6 1.8 convolution_add_fusion.11
  462.7 1.8 convolution_add_fusion.11
  465.9 17.0 %all-gather.2 = f32[8,1,1024]{2,1,0:T(1,128)S(1)} all-gather(f32[1,1,1024]{2,1,0:T(1,128)S(1)} %bitcast.145), channel_id=1, replica_groups=mesh['ctx'=32,'head'=8] {'head'}, dimensions={0}, use_global_device_ids=true | all-gather | bytes 36864 | tf_op jit(solution)/shard_map/all_gather | solution.py:113
  (187 shorter events, 110.1 us)
Async XLA Ops:
  6.5 7.5 %copy-start.4 = (bf16[1024,256]{1,0:T(8,128)(2,1)S(1)}, bf16[1024,256]{1,0:T(8,128)(2,1)}, u32[]{:S(2)}) copy-start(bf16[1024,256]{1,0:T(8,128)(2,1)} %param.13) | copy-start | bytes 1572868
  6.5 289.0 %all-gather.8.cloned.1.call-start = ((), (), s32[]{:S(2)}) async-start(), calls=%async_computation.1 | async-start | bytes 4325376 | tf_op jit(solution)/shard_map/all_gather | solution.py:13
  23.5 163.7 %copy-start.6 = (f32[8,2,128]{2,0,1:T(8,128)S(1)}, f32[8,2,128]{2,0,1:T(8,128)}, u32[]{:S(2)}) copy-start(f32[8,2,128]{2,0,1:T(8,128)} %copy.94) | copy-start | bytes 24580
  187.2 1.9 copy-start.3
  193.7 2.9 copy-start.7
  195.6 1.0 copy-start
  218.8 0.7 copy-start.2
  218.8 0.7 copy-start.1
  218.9 2.6 copy-start.5
  219.5 157.7 %all-gather.6.cloned.1.call-start = ((), (), s32[]{:S(2)}) async-start(), calls=%async_computation | async-start | bytes 4325376 | tf_op jit(solution)/shard_map/all_gather | solution.py:13
  465.7 18.1 %copy-start.8 = (f32[256]{0:T(256)S(1)}, f32[256]{0:T(256)}, u32[]{:S(2)}) copy-start(f32[256]{0:T(256)} %param.17) | copy-start | bytes 3076
Sparse Core Ops, SparseCore 0:
  219.6 75.8 all-gather.7
  298.1 79.0 all-gather.5
